TPU v7x, 32 devices: a whole 2x2x4 slice. The times are simulated.
32 devices in a mesh: fsdp: 16 (over z, y, core), dp: 2 (over x).
Axes of the slice: x: 2, y: 2, z: 4, core: 2. Of those that a mesh axis runs over, the one named last changes fastest.
Arguments:
- acts: bfloat16 [2048, 4096], P(('dp', 'fsdp')), may hold values from -6 to 6
- out_grad: bfloat16 [2048, 4096], P(('dp', 'fsdp')), may hold values from -6 to 6
- gate_weight: bfloat16 [14336, 4096], P('fsdp'), may hold values from -0.09375 to 0.09375
- up_weight: bfloat16 [14336, 4096], P('fsdp'), may hold values from -0.09375 to 0.09375
- proj_in: bfloat16 [14336, 64], P('fsdp'), may hold values from -0.046875 to 0.046875
- proj_out: bfloat16 [4096, 64], replicated, may hold values from -0.09375 to 0.09375
Outputs:
- features: float32 [4, 4096], P('dp', 'fsdp')
- gram: float32 [4096, 4096], P('fsdp', 'dp')
All inputs are finite; a program needn't handle non-finite values.
Results may differ from a plain program's by a relative error of at most 0.0038.
Values may be sent and summed in bfloat16 or wider, within the bound.
A program may use at most 128 MiB of HBM per device.

v0:
```python
import jax
import jax.numpy as jnp
from jax import lax
from jax.sharding import PartitionSpec as P

LEN = 512


def outer_rows(u_part, v_rows):
    return (u_part[:, :, None] * v_rows[:, None, :]).reshape(
        u_part.shape[0], u_part.shape[1] * v_rows.shape[1]
    )


def moment_rows(u_part, u_cols, v_rows):
    a_rows = outer_rows(u_part, v_rows)
    z_cols = outer_rows(u_cols, v_rows)
    return lax.dot_general(
        a_rows,
        z_cols,
        (((0,), (0,)), ((), ())),
        precision=lax.Precision.HIGHEST,
        preferred_element_type=jnp.float32,
    )


def local(acts, out_grad, gate_weight, up_weight, proj_in, proj_out):
    n_fsdp = lax.axis_size("fsdp")
    n_dp = lax.axis_size("dp")
    contract = (((1,), (1,)), ((), ()))
    piece = lax.all_gather(acts, "fsdp", axis=0, tiled=True)
    gate = lax.dot_general(piece, gate_weight, contract, preferred_element_type=jnp.float32)
    upper = lax.dot_general(piece, up_weight, contract, preferred_element_type=jnp.float32)
    hidden = (jax.nn.silu(gate) * upper).astype(jnp.bfloat16)
    part_in = jnp.dot(hidden, proj_in, preferred_element_type=jnp.float32)
    left = lax.psum(part_in, "fsdp")
    part_out = jnp.dot(out_grad, proj_out, preferred_element_type=jnp.float32)
    right = lax.all_gather(part_out, "fsdp", axis=0, tiled=True)
    rows = left.shape[0]
    total_tokens = rows * n_dp
    kp_size = left.shape[1]
    kq_size = right.shape[1]
    row_width = kp_size // n_fsdp
    first = lax.axis_index("fsdp") * row_width
    mine = lax.dynamic_slice_in_dim(left, first, row_width, 1)
    examples = rows // LEN
    left_ex = left.reshape(examples, LEN, kp_size)
    right_ex = right.reshape(examples, LEN, kq_size)
    mine_ex = mine.reshape(examples, LEN, row_width)
    raw = jnp.einsum("elw,elq->ewq", mine_ex, right_ex, precision=lax.Precision.HIGHEST).reshape(
        examples, row_width * kq_size
    )
    squared = lax.psum(jnp.sum(raw * raw, axis=1), "fsdp")
    features = raw / jnp.sqrt(squared + 1e-06)[:, None]

    def add_example(index, total):
        u_rows = lax.dynamic_index_in_dim(left_ex, index, 0, keepdims=False)
        v_rows = lax.dynamic_index_in_dim(right_ex, index, 0, keepdims=False)
        u_part = lax.dynamic_index_in_dim(mine_ex, index, 0, keepdims=False)
        return total + moment_rows(u_part, u_rows, v_rows)

    start_total = jnp.zeros((row_width * kq_size, kp_size * kq_size), jnp.float32)
    partial_value = lax.fori_loop(0, examples, add_example, start_total)
    gram = lax.psum_scatter(
        partial_value / jnp.float32(total_tokens), "dp", scatter_dimension=1, tiled=True
    )
    return (features, gram)


def solution(mesh):
    in_specs = (
        P(("dp", "fsdp"), None),
        P(("dp", "fsdp"), None),
        P("fsdp", None),
        P("fsdp", None),
        P("fsdp", None),
        P(),
    )
    out_specs = (P("dp", "fsdp"), P("fsdp", "dp"))
    return jax.shard_map(local, mesh=mesh, in_specs=in_specs, out_specs=out_specs, check_vma=False)
```

profile of v0, /device:TPU:0, one launch (start us, length us, event | category | flops | bytes accessed | tf_op | source)
XLA Modules:
  0.0 298.4 jit_solution(15123469934350655141)
XLA Ops:
  7.2 0.0 all-gather.2.cloned.1.call-start
  7.2 0.7 all-gather.2.cloned.1.call-update
  7.9 0.0 all-reduce.2.cloned.1.call-start
  8.0 79.8 %all-gather.2.cloned.1.call-done = bf16[1024,4096]{1,0:T(8,128)(2,1)} async-done(((bf16[64,4096]{1,0:T(8,128)(2,1)}), bf16[1024,4096]{1,0:T(8,128)(2,1)}) %all-gather.2.cloned.1.call-update) | async-done | bytes 8388624 | tf_op jit(solution)/shard_map/all_gather | solution.py:31
  87.8 14.6 %fusion.3 = f32[1024,896]{1,0:T(8,128)} fusion(bf16[1024,4096]{1,0:T(8,128)(2,1)} %all-gather.2.cloned.1.call-done, bf16[896,4096]{1,0:T(8,128)(2,1)} %param.10), kind=kOutput, calls=%fused_computation.16 | convolution fusion | flops 7516192768 | bytes 19398656 | tf_op jit(solution)/shard_map/dot_general | solution.py:32
  102.5 15.2 %fusion = f32[1024,64]{0,1:T(8,128)} fusion(bf16[896,64]{0,1:T(8,128)(2,1)S(1)} %copy-done.4, f32[1024,896]{1,0:T(8,128)} %fusion.3, bf16[1024,4096]{1,0:T(8,128)(2,1)} %all-gather.2.cloned.1.call-done, bf16[896,4096]{1,0:T(8,128)(2,1)} %param.11), kind=kOutput, calls=%fused_computation.9 | convolution fusion | flops 7639138304 | bytes 19775488 | tf_op jit(solution)/shard_map/dot_general | solution.py:35
  117.7 0.0 reduce-scatter.2.cloned.1.call-start
  117.8 0.3 fusion.4
  118.1 20.5 %all_gather.7 = f32[1024,64]{1,0:T(8,128)S(1)} all-gather(f32[64,64]{1,0:T(8,128)S(1)} %fusion.4), channel_id=1, replica_groups=mesh['fsdp'=16,'dp'=2] {'fsdp'}, dimensions={0}, use_global_device_ids=true | all-gather | bytes 278528 | tf_op jit(solution)/shard_map/all_gather | solution.py:38
  138.6 0.2 copy.11
  138.8 66.7 %all-reduce.2.cloned.1.call-done = f32[1024,64]{0,1:T(8,128)} async-done(((f32[1024,64]{0,1:T(8,128)}), f32[1024,64]{0,1:T(8,128)}) %all-reduce.2.cloned.1.call-update) | async-done | bytes 262160 | tf_op jit(solution)/shard_map/psum | solution.py:36
  205.5 1.2 reshape.60
  206.7 0.8 constant_dynamic-slice_fusion.1
  207.4 24.8 %while.14 = (s32[]{:T(128)}, f32[256,4096]{1,0:T(8,128)}, f32[2,512,4]{1,2,0:T(4,128)S(1)}, f32[2,512,64]{1,2,0:T(8,128)S(1)}, f32[2,512,64]{1,0,2:T(2,128)S(1)}, /*index=5*/s32[]{:T(128)}, s32[]{:T(128)}) while((s32[]{:T(128)}, f32[256,4096]{1,0:T(8,128)}, f32[2,512,4]{1,2,0:T(4,128)S(1)}, f32[2,512,64]{1,2,0:T(8,128)S(1)}, ...), condition=%wide.region_4.5_spmd.clone, body=%wide.region_3.4_spmd.clone.sunk | while | flops 6446776320 | bytes 60973216 | solution.py:63
  207.4 0.1 constant_dynamic-slice_fusion.3
  207.6 0.1 broadcast_multiply_fusion.5
  207.7 1.1 broadcast_multiply_fusion.6
  208.8 1.1 copy-done.1
  209.8 8.0 %convolution_add_fusion.2 = f32[256,4096]{1,0:T(8,128)S(1)} fusion(f32[512,256]{0,1:T(8,128)S(1)} %bitcast.36, f32[512,4096]{0,1:T(8,128)S(1)} %bitcast.35, f32[256,4096]{1,0:T(8,128)S(1)} %copy-done.1, pred[]{:T(512)S(6)} %compare.3), kind=kOutput, calls=%fused_computation.clone.1 | convolution fusion | flops 6444548096 | bytes 17301504 | tf_op jit(solution)/shard_map/while/body/eval_jaxpr/dot_general | solution.py:18
  217.9 1.9 copy-done.2
  219.8 0.1 constant_dynamic-slice_fusion.3
  220.0 0.1 broadcast_multiply_fusion.5
  220.1 1.1 broadcast_multiply_fusion.6
  221.2 1.1 copy-done.1
  222.2 8.0 %convolution_add_fusion.2 = f32[256,4096]{1,0:T(8,128)S(1)} fusion(f32[512,256]{0,1:T(8,128)S(1)} %bitcast.36, f32[512,4096]{0,1:T(8,128)S(1)} %bitcast.35, f32[256,4096]{1,0:T(8,128)S(1)} %copy-done.1, pred[]{:T(512)S(6)} %compare.3), kind=kOutput, calls=%fused_computation.clone.1 | convolution fusion | flops 6444548096 | bytes 17301504 | tf_op jit(solution)/shard_map/while/body/eval_jaxpr/dot_general | solution.py:18
  230.3 1.9 copy-done.2
  232.2 4.6 %broadcast_multiply_fusion.2 = f32[256,4096]{1,0:T(8,128)} fusion(f32[256,4096]{1,0:T(8,128)} %get-tuple-element.96), kind=kLoop, calls=%fused_computation.8 | loop fusion | flops 1048576 | bytes 8388608 | tf_op jit(solution)/shard_map/div | solution.py:65
  236.9 0.5 multiply_reduce_fusion
  237.3 32.0 %psum.15 = f32[2]{0:T(128)S(1)} all-reduce(f32[2]{0:T(128)S(1)} %get-tuple-element.137), channel_id=1, replica_groups=mesh['fsdp'=16,'dp'=2] {'fsdp'}, use_global_device_ids=true, to_apply=%region_2.3 | all-reduce | flops 2 | bytes 16 | tf_op jit(solution)/shard_map/psum | solution.py:53
  269.3 0.1 reshape.59
  269.4 0.7 broadcast_divide_fusion
  270.1 21.8 %reduce-scatter.2.cloned.1.call-done = f32[256,2048]{1,0:T(8,128)} async-done(((f32[256,4096]{1,0:T(8,128)}), f32[256,2048]{1,0:T(8,128)}) %reduce-scatter.2.cloned.1.call-update) | async-done | bytes 2097168 | tf_op jit(solution)/shard_map/reduce_scatter | solution.py:64
  (18 shorter events, 0.1 us)
Async XLA Ops:
  7.2 110.6 %copy-start = (bf16[64,4096]{1,0:T(8,128)(2,1)S(1)}, bf16[64,4096]{1,0:T(8,128)(2,1)}, u32[]{:S(2)}) copy-start(bf16[64,4096]{1,0:T(8,128)(2,1)} %param.9) | copy-start | bytes 1572868
  7.2 80.6 %all-gather.2.cloned.1.call-start = ((), (), s32[]{:S(2)}) async-start(), calls=%async_computation.1 | async-start | bytes 8912896 | tf_op jit(solution)/shard_map/all_gather | solution.py:31
  7.9 94.5 %copy-start.4 = (bf16[896,64]{0,1:T(8,128)(2,1)S(1)}, bf16[896,64]{0,1:T(8,128)(2,1)}, u32[]{:S(2)}) copy-start(bf16[896,64]{0,1:T(8,128)(2,1)} %param.12) | copy-start | bytes 344068
  7.9 197.6 %all-reduce.2.cloned.1.call-start = ((), (), s32[]{:S(2)}) async-start(), calls=%async_computation.2 | async-start | bytes 524288 | tf_op jit(solution)/shard_map/psum | solution.py:36
  102.5 15.3 %copy-start.3 = (bf16[4096,64]{0,1:T(8,128)(2,1)S(1)}, bf16[4096,64]{0,1:T(8,128)(2,1)}, u32[]{:S(2)}) copy-start(bf16[4096,64]{0,1:T(8,128)(2,1)} %param.13) | copy-start | bytes 1572868
  117.7 174.1 %reduce-scatter.2.cloned.1.call-start = ((), (), s32[]{:S(2)}) async-start(), calls=%async_computation.3 | async-start | bytes 6291456 | tf_op jit(solution)/shard_map/reduce_scatter | solution.py:64
  207.7 2.2 copy-start.1
  217.9 1.9 copy-start.2
  220.1 2.2 copy-start.1
  230.3 1.9 copy-start.2
Sparse Core Ops, SparseCore 0:
  10.2 77.5 all-gather.1
  117.8 87.6 all-reduce.1
  237.0 54.7 reduce-scatter.1
where the time goes:
time: 299 us; the launch traced here: 298 us
  waiting for transfers between devices  169 us (57%)
  blocking collectives  52.5 us (18%)
  matrix products  46.7 us (16%)
  between operations  13.8 us (5%)
  local copies, waits for them, and re-layouts  8.52 us (3%)
  other arithmetic  7.58 us (3%)
    all_gather x1, waiting for transfers between devices, local(): piece = lax.all_gather(acts, 'fsdp', axis=0, tiled=True)  79.8 us
    psum x1, waiting for transfers between devices, local(): left = lax.psum(part_in, 'fsdp')  66.7 us
    psum x1, blocking collectives, local(): squared = lax.psum(jnp.sum(raw * raw, axis=1), 'fsdp')  32 us
    reduce_scatter x1, waiting for transfers between devices, local(): lax.psum_scatter(partial_value / jnp.float32(total_tokens), 'dp', scatter...  21.8 us
    all_gather x1, blocking collectives, local(): right = lax.all_gather(part_out, 'fsdp', axis=0, tiled=True)  20.5 us
    dot_general x2, matrix products, moment_rows(): lax.dot_general(a_rows, z_cols, (((0,), (0,)), ((), ())), precision=lax.P...  16.1 us
    dot_general x1, matrix products, local(): part_in = jnp.dot(hidden, proj_in, preferred_element_type=jnp.float32)  15.2 us
    dot_general x1, matrix products, local(): lax.dot_general(piece, gate_weight, contract, preferred_element_type=jnp....  14.6 us
  transfers between devices with their start and end apart: 3, of which 3 were waited for; matrix products, arithmetic and copies ran while one was open for 1% of the time, Pallas kernels for 0%

commit v1 on v0

--- a/solution.py
+++ b/solution.py
@@ -1,6 +1,10 @@
+import functools
+
 import jax
 import jax.numpy as jnp
 from jax import lax
+from jax.experimental import pallas as pl
+from jax.experimental.pallas import tpu as pltpu
 from jax.sharding import PartitionSpec as P
 
 LEN = 512
@@ -67,7 +71,314 @@
     return (features, gram)
 
 
+MESH = pl.DeviceIdType.MESH
+NT = (((1,), (1,)), ((), ()))
+NN = (((1,), (0,)), ((), ()))
+F32 = jnp.float32
+BF16 = jnp.bfloat16
+PLANE = 4
+
+
+def fused_kernel(n_f, n_dp, acts, out_grad, gate_w, up_w, proj_in, proj_out, feat, gram,
+                 xbuf, wbuf, pin, og, part, lrecv, rbuf, lbuf, ut, vt, raw_s,
+                 own_sem, w_sem, zr_sem, yr_sem, cr_sem, zu_s, zd_s, ys_s, cs_s,
+                 part_s, part_r, r_s, r_r, l_s, l_r):
+    n_z = n_f // PLANE
+    n_all = n_f * n_dp
+    rows = acts.shape[0]
+    units = gate_w.shape[0]
+    n_chunk = units // 128
+    prow = rows * PLANE
+    kp = proj_in.shape[0]
+    kq = proj_out.shape[0]
+    d = lax.axis_index("dp")
+    f = lax.axis_index("fsdp")
+    g = d * n_f + f
+    z = f // PLANE
+    y = (f // 2) % 2
+    c = f % 2
+    h = g // 2
+    n_chip = n_all // 2
+
+    def at(fi):
+        return {"dp": d, "fsdp": fi}
+
+    def device(gi):
+        return {"dp": gi // n_f, "fsdp": gi % n_f}
+
+    own = pltpu.make_async_copy(acts, xbuf.at[f], own_sem.at[0])
+    own.start()
+    ogc = pltpu.make_async_copy(out_grad, og, own_sem.at[1])
+    ogc.start()
+    weights = []
+    for k in range(n_chunk):
+        for s, w in enumerate((gate_w, up_w)):
+            cp = pltpu.make_async_copy(
+                w.at[pl.ds(128 * k, 128)], wbuf.at[k, pl.ds(128 * s, 128)], w_sem.at[2 * k + s]
+            )
+            cp.start()
+            weights.append(cp)
+
+    barrier = pltpu.get_barrier_semaphore()
+
+    def greet(o, carry):
+        pl.semaphore_signal(barrier, inc=1, device_id=device((g + o) % n_all), device_id_type=MESH)
+        return carry
+
+    lax.fori_loop(1, n_all, greet, 0)
+    pl.semaphore_wait(barrier, n_all - 1)
+
+    def push(block, target, send, recv):
+        return pltpu.make_async_remote_copy(
+            src_ref=xbuf.at[block], dst_ref=xbuf.at[block], send_sem=send, recv_sem=recv,
+            device_id=at(target), device_id_type=MESH,
+        )
+
+    def z_up(p):
+        return push(p * PLANE + y * 2 + c, f + PLANE, zu_s.at[p], zr_sem.at[p])
+
+    def z_down(p):
+        return push(p * PLANE + y * 2 + c, f - PLANE, zd_s.at[p], zr_sem.at[p])
+
+    def y_send(p):
+        return push(p * PLANE + y * 2 + c, z * PLANE + (1 - y) * 2 + c, ys_s.at[p], yr_sem.at[p])
+
+    def c_send(p, yy):
+        return push(p * PLANE + yy * 2 + c, z * PLANE + y * 2 + 1 - c, cs_s.at[2 * p + yy], cr_sem.at[2 * p + yy])
+
+    def when(cond, fn):
+        if cond is None:
+            fn()
+        else:
+            pl.when(cond)(fn)
+
+    def planes(r):
+        if r == 0:
+            return [(z, None, 0)]
+        return [(z - r, z - r >= 0, 1), (z + r, z + r < n_z, -1)]
+
+    def spread(r):
+        for p, ok, way in planes(r):
+            def go(p=p, way=way):
+                if way != 0:
+                    z_up(p).wait_recv()
+                if way >= 0:
+                    pl.when(z < n_z - 1)(lambda: z_up(p).start())
+                if way <= 0:
+                    pl.when(z > 0)(lambda: z_down(p).start())
+                y_send(p).start()
+                c_send(p, y).start()
+            when(ok, go)
+
+    def part_copy(p, q):
+        return pltpu.make_async_remote_copy(
+            src_ref=part.at[p, pl.ds(16 * q, 16)], dst_ref=lrecv.at[f],
+            send_sem=part_s.at[p * PLANE + q], recv_sem=part_r.at[f],
+            device_id=at(p * PLANE + q), device_id_type=MESH,
+        )
+
+    def work(r):
+        for p, ok, _ in planes(r):
+            def relay(p=p):
+                y_send(p).wait_recv()
+                c_send(p, 1 - y).start()
+            when(ok, relay)
+        for p, ok, _ in planes(r):
+            def go(p=p):
+                c_send(p, 0).wait_recv()
+                c_send(p, 1).wait_recv()
+
+                def chunk(k, total):
+                    x = xbuf[pl.ds(p * PLANE, PLANE)].reshape(prow, acts.shape[1])
+                    both = lax.dot_general(wbuf[k], x, NT, preferred_element_type=F32)
+                    gate = both[:128]
+                    hidden = (gate / (1.0 + jnp.exp(-gate)) * both[128:]).astype(BF16)
+                    return total + lax.dot_general(pin[k], hidden, NN, preferred_element_type=F32)
+
+                total = lax.fori_loop(0, n_chunk, chunk, jnp.zeros((kp, prow), F32))
+                part[p] = total
+                for q in range(PLANE):
+                    mine = p * PLANE + q == f
+                    pl.when(jnp.logical_not(mine))(lambda q=q: part_copy(p, q).start())
+
+                    def keep(q=q):
+                        lrecv[f] = part[p, pl.ds(16 * q, 16)]
+                    pl.when(mine)(keep)
+            when(ok, go)
+
+    own.wait()
+    spread(0)
+
+    ogc.wait()
+    for k in range(n_chunk):
+        pin[k] = proj_in[:, pl.ds(128 * k, 128)]
+    right = lax.dot_general(og[...], proj_out[...], NT, preferred_element_type=F32)
+    rbuf[c, h] = jnp.concatenate([right[:rows // 2], right[rows // 2:]], axis=1)
+
+    def share(buf, send, recv, o):
+        return pltpu.make_async_remote_copy(
+            src_ref=buf.at[c, h], dst_ref=buf.at[c, h], send_sem=send.at[o], recv_sem=recv.at[o],
+            device_id=device(((h + o) % n_chip) * 2 + c), device_id_type=MESH,
+        )
+
+    def swap(buf, send, recv):
+        return pltpu.make_async_remote_copy(
+            src_ref=buf.at[c], dst_ref=buf.at[c], send_sem=send.at[0], recv_sem=recv.at[0],
+            device_id=at(f + 1 - 2 * c), device_id_type=MESH,
+        )
+
+    def each(fn):
+        def body(o, carry):
+            fn(o)
+            return carry
+        lax.fori_loop(1, n_chip, body, 0)
+
+    each(lambda o: share(rbuf, r_s, r_r, o).start())
+    for cp in weights:
+        cp.wait()
+
+    for r in range(1, n_z):
+        spread(r)
+        work(r - 1)
+        if r == 1:
+            each(lambda o: share(rbuf, r_s, r_r, o).wait())
+            swap(rbuf, r_s, r_r).start()
+
+    swap(rbuf, r_s, r_r).wait()
+    lane = lax.broadcasted_iota(jnp.int32, (kq, 2 * rows), 1)
+    low = lane // (rows // 2) % 2 == 0
+    for b in range(n_chip):
+        one, two = rbuf[0, b], rbuf[1, b]
+        tall = jnp.concatenate([one, one, two, two], axis=0).T
+        vt[:, pl.ds(2 * rows * b, 2 * rows)] = jnp.where(low, tall[:kq], tall[kq:])
+    work(n_z - 1)
+
+    def wait_part(s, carry):
+        def go():
+            pltpu.make_async_remote_copy(
+                src_ref=lrecv.at[s], dst_ref=lrecv.at[s], send_sem=part_s.at[s], recv_sem=part_r.at[s],
+                device_id=at(f), device_id_type=MESH,
+            ).wait_recv()
+        pl.when(s != f)(go)
+        return carry
+
+    lax.fori_loop(0, n_f, wait_part, 0)
+    total = lrecv[0]
+    for s in range(1, n_f):
+        total = total + lrecv[s]
+    lbuf[c, h] = total
+    each(lambda o: share(lbuf, l_s, l_r, o).start())
+    each(lambda o: share(lbuf, l_s, l_r, o).wait())
+    swap(lbuf, l_s, l_r).start()
+    swap(lbuf, l_s, l_r).wait()
+
+    for b in range(n_all):
+        q = b % PLANE
+        tok = (b // n_f) * n_z + (b % n_f) // PLANE
+        ut[pl.ds(16 * q, 16), pl.ds(prow * tok, prow)] = lbuf[b % 2, b // 2]
+
+    width = kp // n_f
+    cols = kp // n_dp
+    tokens = ut.shape[1]
+    group = tokens // n_dp
+
+    def z_rows(first, count):
+        v = vt[...]
+        return jnp.concatenate([(ut[pl.ds(first + i, 1), :] * v).astype(BF16) for i in range(count)], axis=0)
+
+    a_rows = z_rows(f * width, width)
+    for k in range(cols // 4):
+        z_cols = z_rows(d * cols + 4 * k, 4)
+        block = lax.dot_general(a_rows, z_cols, NT, preferred_element_type=F32)
+        gram[:, pl.ds(4 * kq * k, 4 * kq)] = block * (1.0 / tokens)
+
+    for e in range(group // LEN):
+        span = pl.ds(pl.multiple_of(d * group + e * LEN, LEN), LEN)
+        raw = lax.dot_general(ut[:, span], vt[:, span], NT, precision=lax.Precision.HIGHEST, preferred_element_type=F32)
+        norm = jnp.sqrt(jnp.sum(raw * raw, keepdims=True) + 1e-06)
+        raw_s[...] = raw / norm
+        for i in range(width):
+            feat[e, pl.ds(i, 1), :] = raw_s[pl.ds(f * width + i, 1), :]
+
+    for r in range(n_z):
+        for p, ok, way in planes(r):
+            def fin(p=p, way=way):
+                if way >= 0:
+                    pl.when(z < n_z - 1)(lambda: z_up(p).wait_send())
+                if way <= 0:
+                    pl.when(z > 0)(lambda: z_down(p).wait_send())
+                y_send(p).wait_send()
+                c_send(p, 0).wait_send()
+                c_send(p, 1).wait_send()
+                for q in range(PLANE):
+                    pl.when(p * PLANE + q != f)(lambda q=q: part_copy(p, q).wait_send())
+            when(ok, fin)
+
+
+def fused(n_f, n_dp, acts, out_grad, gate_weight, up_weight, proj_in, proj_out):
+    rows, depth = acts.shape
+    units = gate_weight.shape[0]
+    kp, kq = proj_in.shape[1], proj_out.shape[1]
+    n_all = n_f * n_dp
+    tokens = rows * n_all
+    n_chunk = units // 128
+    n_z = n_f // PLANE
+    width = kp // n_f
+    examples = rows * n_f // LEN
+    dma = pltpu.SemaphoreType.DMA
+    hbm = pl.BlockSpec(memory_space=pl.ANY)
+    vmem = pl.BlockSpec(memory_space=pltpu.VMEM)
+    features, gram = pl.pallas_call(
+        functools.partial(fused_kernel, n_f, n_dp),
+        out_shape=(
+            jax.ShapeDtypeStruct((examples, width, kq), F32),
+            jax.ShapeDtypeStruct((width * kq, kp * kq // n_dp), F32),
+        ),
+        in_specs=[hbm, hbm, hbm, hbm, vmem, vmem],
+        out_specs=(vmem, vmem),
+        scratch_shapes=[
+            pltpu.VMEM((n_f, rows, depth), BF16),
+            pltpu.VMEM((n_chunk, 256, depth), BF16),
+            pltpu.VMEM((n_chunk, kp, 128), BF16),
+            pltpu.VMEM((rows, depth), BF16),
+            pltpu.VMEM((n_z, kp, rows * PLANE), F32),
+            pltpu.VMEM((n_f, 16, rows * PLANE), F32),
+            pltpu.VMEM((2, n_all // 2, rows // 2, 2 * kq), F32),
+            pltpu.VMEM((2, n_all // 2, 16, rows * PLANE), F32),
+            pltpu.VMEM((kp, tokens), F32),
+            pltpu.VMEM((kq, tokens), F32),
+            pltpu.VMEM((kp, kq), F32),
+            dma((2,)), dma((2 * n_chunk,)), dma((n_z,)), dma((n_z,)), dma((2 * n_z,)),
+            dma((n_z,)), dma((n_z,)), dma((n_z,)), dma((2 * n_z,)),
+            dma((n_f,)), dma((n_f,)), dma((n_all // 2,)), dma((n_all // 2,)), dma((n_all // 2,)), dma((n_all // 2,)),
+        ],
+        compiler_params=pltpu.CompilerParams(
+            collective_id=0, has_side_effects=True, vmem_limit_bytes=56 * 1024 * 1024
+        ),
+    )(acts, out_grad, gate_weight, up_weight, proj_in.T, proj_out.T)
+    return features.reshape(examples, width * kq), gram
+
+
 def solution(mesh):
+    n_f, n_dp = mesh.shape["fsdp"], mesh.shape["dp"]
+
+    def run(acts, out_grad, gate_weight, up_weight, proj_in, proj_out):
+        rows, units = acts.shape[0], gate_weight.shape[0]
+        fits = (
+            n_f % PLANE == 0
+            and (PLANE * rows) % 128 == 0
+            and units % 128 == 0
+            and proj_out.shape[1] == 64
+            and (2 * rows) % 128 == 0
+            and proj_in.shape[1] == 16 * PLANE
+            and proj_in.shape[1] % n_f == 0
+            and proj_in.shape[1] % (4 * n_dp) == 0
+            and (rows * n_f) % LEN == 0
+        )
+        if fits:
+            return fused(n_f, n_dp, acts, out_grad, gate_weight, up_weight, proj_in, proj_out)
+        return local(acts, out_grad, gate_weight, up_weight, proj_in, proj_out)
+
     in_specs = (
         P(("dp", "fsdp"), None),
         P(("dp", "fsdp"), None),
@@ -77,4 +388,4 @@
         P(),
     )
     out_specs = (P("dp", "fsdp"), P("fsdp", "dp"))
-    return jax.shard_map(local, mesh=mesh, in_specs=in_specs, out_specs=out_specs, check_vma=False)
+    return jax.shard_map(run, mesh=mesh, in_specs=in_specs, out_specs=out_specs, check_vma=False)

time: 299 us -> 94.6 us (0.32)
  waiting for transfers between devices: 169 us -> 0 us
  Pallas kernels: 0 us -> 89.3 us
  blocking collectives: 52.5 us -> 0 us
  matrix products: 46.7 us -> 0 us
  between operations: 13.8 us -> 0.64 us
  other arithmetic: 7.58 us -> 0 us
  local copies, waits for them, and re-layouts: 8.52 us -> 4.47 us
    pallas_call x0 -> x1, Pallas kernels: none -> 89.3 us  [fused(): pl.pallas_call(functools.partial(fused_kernel, n_f, n_dp), out_shape=(jax...]
    all_gather x1 -> x0, waiting for transfers between devices: 79.8 us -> none  [local(): piece = lax.all_gather(acts, 'fsdp', axis=0, tiled=True)]
    psum x1 -> x0, waiting for transfers between devices: 66.7 us -> none  [local(): left = lax.psum(part_in, 'fsdp')]
    dot_general x6 -> x0, matrix products: 46.7 us -> none  [the longest x2 16.1 us: moment_rows(): lax.dot_general(a_rows, z_cols, (((0,), (0,)), ((), ())), precision=lax.P...]
    psum x1 -> x0, blocking collectives: 32 us -> none  [local(): squared = lax.psum(jnp.sum(raw * raw, axis=1), 'fsdp')]
    reduce_scatter x1 -> x0, waiting for transfers between devices: 21.8 us -> none  [local(): lax.psum_scatter(partial_value / jnp.float32(total_tokens), 'dp', scatter...]
    all_gather x1 -> x0, blocking collectives: 20.5 us -> none  [local(): right = lax.all_gather(part_out, 'fsdp', axis=0, tiled=True)]
    while x8 -> x0, local copies, waits for them, and re-layouts: 6.02 us -> none
  transfers between devices with their start and end apart: 3 -> 0, of which waited for: 3 -> 0; matrix products, arithmetic and copies ran while one was open for 1% -> 0% of each run, Pallas kernels for 0% -> 0%
where the time goes in v1:
time: 94.6 us; the launch traced here: 94.4 us
  Pallas kernels  89.3 us (94%)
  local copies, waits for them, and re-layouts  4.47 us (5%)
    pallas_call x1, Pallas kernels, fused(): pl.pallas_call(functools.partial(fused_kernel, n_f, n_dp), out_shape=(jax...  89.3 us
    unnamed x1, local copies, waits for them, and re-layouts  3.13 us

profile of v1, /device:TPU:0, one launch (start us, length us, event | category | flops | bytes accessed | tf_op | source)
XLA Modules:
  0.0 94.4 jit_solution(278346233962332603)
XLA Ops:
  0.6 89.3 %shard_map.77 = (f32[2,4,64]{2,1,0:T(4,128)}, f32[256,2048]{1,0:T(8,128)}) custom-call(bf16[64,4096]{1,0:T(8,128)(2,1)} %acts.1, bf16[64,4096]{1,0:T(8,128)(2,1)} %out_grad.1, bf16[896,4096]{1,0:T(8,128)(2,1)} %gate_w.1, bf16[896,4096]{1,0:T(8,128)(2,1)} %up_w.1, bf16[64,896]{1,0:T(8,128)(2,1)} %bitcast.3, bf16[64,4096]{1,0:T(8,128)(2,1)} %bitcast.2), custom_call_target="tpu_custom_call" | custom-call | tf_op jit(solution)/shard_map/pallas_call | solution.py:331
  90.0 1.3 %reshape.7 = f32[2,256]{1,0:T(2,128)} reshape(f32[2,4,64]{2,1,0:T(4,128)} %get-tuple-element.4) | data formatting | bytes 4096 | tf_op jit(solution)/shard_map/reshape | solution.py:359
  91.3 3.1 %copy.9 = f32[256,2048]{1,0:T(8,128)} copy(f32[256,2048]{1,0:T(8,128)} %get-tuple-element.9) | data formatting | bytes 4194304

commit v2 on v1

--- a/solution.py
+++ b/solution.py
@@ -79,9 +79,9 @@
 PLANE = 4
 
 
-def fused_kernel(n_f, n_dp, acts, out_grad, gate_w, up_w, proj_in, proj_out, feat, gram,
-                 xbuf, wbuf, pin, og, part, lrecv, rbuf, lbuf, ut, vt, raw_s,
-                 own_sem, w_sem, zr_sem, yr_sem, cr_sem, zu_s, zd_s, ys_s, cs_s,
+def fused_kernel(n_f, n_dp, acts, out_grad, gate_w, up_w, proj_in, proj_out, ut, vt,
+                 xbuf, wbuf, pin, og, part, lrecv, rbuf, lbuf,
+                 own_sem, w_sem, zr_sem, yr_sem, cr_sem, zu_s, zd_s, ys_s, cs_s, w_s, w_r,
                  part_s, part_r, r_s, r_r, l_s, l_r):
     n_z = n_f // PLANE
     n_all = n_f * n_dp
@@ -143,6 +143,33 @@
     def y_send(p):
         return push(p * PLANE + y * 2 + c, z * PLANE + (1 - y) * 2 + c, ys_s.at[p], yr_sem.at[p])
 
+    half = rows // 2
+
+    def y_half(p):
+        block = p * PLANE + y * 2 + c
+        return pltpu.make_async_remote_copy(
+            src_ref=xbuf.at[block, pl.ds(half, half)], dst_ref=xbuf.at[block, pl.ds(half, half)],
+            send_sem=ys_s.at[p], recv_sem=yr_sem.at[p],
+            device_id=at(z * PLANE + (1 - y) * 2 + c), device_id_type=MESH,
+        )
+
+    def w_send(p, step):
+        block = p * PLANE + (1 - y) * 2 + c
+        return pltpu.make_async_remote_copy(
+            src_ref=xbuf.at[block, pl.ds(0, half)], dst_ref=xbuf.at[block, pl.ds(0, half)],
+            send_sem=w_s.at[p], recv_sem=w_r.at[p],
+            device_id=at(f + step * PLANE), device_id_type=MESH,
+        )
+
+    def by_y(p, fn):
+        parted = (p != z) & ((p == 0) | (p == n_z - 1))
+        pl.when(parted)(lambda: fn(y_half(p)))
+        pl.when(jnp.logical_not(parted))(lambda: fn(y_send(p)))
+
+    def by_w(p, fn):
+        pl.when((p == 0) & (z < n_z - 1))(lambda: fn(w_send(p, 1)))
+        pl.when((p == n_z - 1) & (z > 0))(lambda: fn(w_send(p, -1)))
+
     def c_send(p, yy):
         return push(p * PLANE + yy * 2 + c, z * PLANE + y * 2 + 1 - c, cs_s.at[2 * p + yy], cr_sem.at[2 * p + yy])
 
@@ -166,7 +193,7 @@
                     pl.when(z < n_z - 1)(lambda: z_up(p).start())
                 if way <= 0:
                     pl.when(z > 0)(lambda: z_down(p).start())
-                y_send(p).start()
+                by_y(p, lambda cp: cp.start())
                 c_send(p, y).start()
             when(ok, go)
 
@@ -180,7 +207,9 @@
     def work(r):
         for p, ok, _ in planes(r):
             def relay(p=p):
-                y_send(p).wait_recv()
+                by_y(p, lambda cp: cp.wait_recv())
+                pl.when((p != z) & ((p == 0) | (p == n_z - 1)))(lambda: w_send(p, 0).wait_recv())
+                by_w(p, lambda cp: cp.start())
                 c_send(p, 1 - y).start()
             when(ok, relay)
         for p, ok, _ in planes(r):
@@ -266,7 +295,7 @@
     total = lrecv[0]
     for s in range(1, n_f):
         total = total + lrecv[s]
-    lbuf[c, h] = total
+    lbuf[c, h] = total.astype(BF16)
     each(lambda o: share(lbuf, l_s, l_r, o).start())
     each(lambda o: share(lbuf, l_s, l_r, o).wait())
     swap(lbuf, l_s, l_r).start()
@@ -275,30 +304,7 @@
     for b in range(n_all):
         q = b % PLANE
         tok = (b // n_f) * n_z + (b % n_f) // PLANE
-        ut[pl.ds(16 * q, 16), pl.ds(prow * tok, prow)] = lbuf[b % 2, b // 2]
-
-    width = kp // n_f
-    cols = kp // n_dp
-    tokens = ut.shape[1]
-    group = tokens // n_dp
-
-    def z_rows(first, count):
-        v = vt[...]
-        return jnp.concatenate([(ut[pl.ds(first + i, 1), :] * v).astype(BF16) for i in range(count)], axis=0)
-
-    a_rows = z_rows(f * width, width)
-    for k in range(cols // 4):
-        z_cols = z_rows(d * cols + 4 * k, 4)
-        block = lax.dot_general(a_rows, z_cols, NT, preferred_element_type=F32)
-        gram[:, pl.ds(4 * kq * k, 4 * kq)] = block * (1.0 / tokens)
-
-    for e in range(group // LEN):
-        span = pl.ds(pl.multiple_of(d * group + e * LEN, LEN), LEN)
-        raw = lax.dot_general(ut[:, span], vt[:, span], NT, precision=lax.Precision.HIGHEST, preferred_element_type=F32)
-        norm = jnp.sqrt(jnp.sum(raw * raw, keepdims=True) + 1e-06)
-        raw_s[...] = raw / norm
-        for i in range(width):
-            feat[e, pl.ds(i, 1), :] = raw_s[pl.ds(f * width + i, 1), :]
+        ut[pl.ds(16 * q, 16), pl.ds(prow * tok, prow)] = lbuf[b % 2, b // 2].astype(F32)
 
     for r in range(n_z):
         for p, ok, way in planes(r):
@@ -307,12 +313,38 @@
                     pl.when(z < n_z - 1)(lambda: z_up(p).wait_send())
                 if way <= 0:
                     pl.when(z > 0)(lambda: z_down(p).wait_send())
-                y_send(p).wait_send()
+                by_y(p, lambda cp: cp.wait_send())
+                by_w(p, lambda cp: cp.wait_send())
                 c_send(p, 0).wait_send()
                 c_send(p, 1).wait_send()
                 for q in range(PLANE):
                     pl.when(p * PLANE + q != f)(lambda q=q: part_copy(p, q).wait_send())
             when(ok, fin)
+
+
+def moment_kernel(width, cols, group, ut, vt, feat, gram, a_rows, raw_s):
+    k = pl.program_id(0)
+    d = lax.axis_index("dp")
+    f = lax.axis_index("fsdp")
+    tokens = ut.shape[1]
+    kq = vt.shape[0]
+
+    def z_rows(first, count):
+        v = vt[...]
+        return jnp.concatenate([(ut[pl.ds(first + i, 1), :] * v).astype(BF16) for i in range(count)], axis=0)
+
+    def head():
+        a_rows[...] = z_rows(f * width, width)
+        for e in range(group // LEN):
+            span = pl.ds(pl.multiple_of(d * group + e * LEN, LEN), LEN)
+            raw = lax.dot_general(ut[:, span], vt[:, span], NT, precision=lax.Precision.HIGHEST, preferred_element_type=F32)
+            raw_s[...] = raw / jnp.sqrt(jnp.sum(raw * raw, keepdims=True) + 1e-06)
+            for i in range(width):
+                feat[pl.ds(e, 1), pl.ds(kq * i, kq)] = raw_s[pl.ds(f * width + i, 1), :]
+
+    pl.when(k == 0)(head)
+    block = lax.dot_general(a_rows[...], z_rows(d * cols + 4 * k, 4), NT, preferred_element_type=F32)
+    gram[...] = block * (1.0 / tokens)
 
 
 def fused(n_f, n_dp, acts, out_grad, gate_weight, up_weight, proj_in, proj_out):
@@ -328,11 +360,11 @@
     dma = pltpu.SemaphoreType.DMA
     hbm = pl.BlockSpec(memory_space=pl.ANY)
     vmem = pl.BlockSpec(memory_space=pltpu.VMEM)
-    features, gram = pl.pallas_call(
+    ut, vt = pl.pallas_call(
         functools.partial(fused_kernel, n_f, n_dp),
         out_shape=(
-            jax.ShapeDtypeStruct((examples, width, kq), F32),
-            jax.ShapeDtypeStruct((width * kq, kp * kq // n_dp), F32),
+            jax.ShapeDtypeStruct((kp, tokens), F32),
+            jax.ShapeDtypeStruct((kq, tokens), F32),
         ),
         in_specs=[hbm, hbm, hbm, hbm, vmem, vmem],
         out_specs=(vmem, vmem),
@@ -344,19 +376,32 @@
             pltpu.VMEM((n_z, kp, rows * PLANE), F32),
             pltpu.VMEM((n_f, 16, rows * PLANE), F32),
             pltpu.VMEM((2, n_all // 2, rows // 2, 2 * kq), F32),
-            pltpu.VMEM((2, n_all // 2, 16, rows * PLANE), F32),
-            pltpu.VMEM((kp, tokens), F32),
-            pltpu.VMEM((kq, tokens), F32),
-            pltpu.VMEM((kp, kq), F32),
+            pltpu.VMEM((2, n_all // 2, 16, rows * PLANE), BF16),
             dma((2,)), dma((2 * n_chunk,)), dma((n_z,)), dma((n_z,)), dma((2 * n_z,)),
-            dma((n_z,)), dma((n_z,)), dma((n_z,)), dma((2 * n_z,)),
+            dma((n_z,)), dma((n_z,)), dma((n_z,)), dma((2 * n_z,)), dma((n_z,)), dma((n_z,)),
             dma((n_f,)), dma((n_f,)), dma((n_all // 2,)), dma((n_all // 2,)), dma((n_all // 2,)), dma((n_all // 2,)),
         ],
         compiler_params=pltpu.CompilerParams(
             collective_id=0, has_side_effects=True, vmem_limit_bytes=56 * 1024 * 1024
         ),
     )(acts, out_grad, gate_weight, up_weight, proj_in.T, proj_out.T)
-    return features.reshape(examples, width * kq), gram
+    cols = kp // n_dp
+    whole = lambda k: (0, 0)
+    return pl.pallas_call(
+        functools.partial(moment_kernel, width, cols, tokens // n_dp),
+        grid=(cols // 4,),
+        out_shape=(
+            jax.ShapeDtypeStruct((examples, width * kq), F32),
+            jax.ShapeDtypeStruct((width * kq, cols * kq), F32),
+        ),
+        in_specs=[pl.BlockSpec((kp, tokens), whole), pl.BlockSpec((kq, tokens), whole)],
+        out_specs=(
+            pl.BlockSpec((examples, width * kq), whole),
+            pl.BlockSpec((width * kq, 4 * kq), lambda k: (0, k)),
+        ),
+        scratch_shapes=[pltpu.VMEM((width * kq, tokens), BF16), pltpu.VMEM((kp, kq), F32)],
+        compiler_params=pltpu.CompilerParams(vmem_limit_bytes=24 * 1024 * 1024),
+    )(ut, vt)
 
 
 def solution(mesh):
@@ -367,6 +412,7 @@
         fits = (
             n_f % PLANE == 0
             and (PLANE * rows) % 128 == 0
+            and rows % 32 == 0
             and units % 128 == 0
             and proj_out.shape[1] == 64
             and (2 * rows) % 128 == 0

time: 94.6 us -> 92.2 us (0.975)
  local copies, waits for them, and re-layouts: 4.47 us -> 2.08 us
    pallas_call x1, Pallas kernels: 89.3 us -> 83.2 us  [fused(): pl.pallas_call(functools.partial(fused_kernel, n_f, n_dp), out_shape=(jax...]
    pallas_call x0 -> x1, Pallas kernels: none -> 6.06 us  [fused(): pl.pallas_call(functools.partial(moment_kernel, width, cols, tokens // n_...]
    reshape x1 -> x0, local copies, waits for them, and re-layouts: 1.33 us -> none  [fused(): return (features.reshape(examples, width * kq), gram)]
    unnamed x1 -> x4, local copies, waits for them, and re-layouts: 3.13 us -> 2.08 us
where the time goes in v2:
time: 92.2 us; the launch traced here: 92 us
  Pallas kernels  89.2 us (97%)
  local copies, waits for them, and re-layouts  2.08 us (2%)
    pallas_call x1, Pallas kernels, fused(): pl.pallas_call(functools.partial(fused_kernel, n_f, n_dp), out_shape=(jax...  83.2 us
    pallas_call x1, Pallas kernels, fused(): pl.pallas_call(functools.partial(moment_kernel, width, cols, tokens // n_...  6.06 us
    unnamed x4, local copies, waits for them, and re-layouts  2.08 us

profile of v2, /device:TPU:0, one launch (start us, length us, event | category | flops | bytes accessed | tf_op | source)
XLA Modules:
  0.0 92.0 jit_solution(13519944122999604333)
XLA Ops:
  0.6 83.2 %shard_map.77 = (f32[64,2048]{1,0:T(8,128)}, f32[64,2048]{1,0:T(8,128)}) custom-call(bf16[64,4096]{1,0:T(8,128)(2,1)} %acts.1, bf16[64,4096]{1,0:T(8,128)(2,1)} %out_grad.1, bf16[896,4096]{1,0:T(8,128)(2,1)} %gate_w.1, bf16[896,4096]{1,0:T(8,128)(2,1)} %up_w.1, bf16[64,896]{1,0:T(8,128)(2,1)} %bitcast.3, bf16[64,4096]{1,0:T(8,128)(2,1)} %bitcast.2), custom_call_target="tpu_custom_call" | custom-call | tf_op jit(solution)/shard_map/pallas_call | solution.py:363
  83.8 0.0 copy-start
  83.8 1.0 %copy-done = f32[64,2048]{1,0:T(8,128)S(1)} copy-done((f32[64,2048]{1,0:T(8,128)S(1)}, f32[64,2048]{1,0:T(8,128)}, u32[]{:S(2)}) %copy-start) | copy-done | bytes 524312
  84.9 0.0 copy-start.1
  84.9 1.0 %copy-done.1 = f32[64,2048]{1,0:T(8,128)S(1)} copy-done((f32[64,2048]{1,0:T(8,128)S(1)}, f32[64,2048]{1,0:T(8,128)}, u32[]{:S(2)}) %copy-start.1) | copy-done | bytes 524312
  85.9 6.1 %shard_map.78 = (f32[2,256]{1,0:T(2,128)}, f32[256,2048]{1,0:T(8,128)}) custom-call(f32[64,2048]{1,0:T(8,128)S(1)} %copy-done, f32[64,2048]{1,0:T(8,128)S(1)} %copy-done.1), custom_call_target="tpu_custom_call" | custom-call | tf_op jit(solution)/shard_map/pallas_call | solution.py:390
Async XLA Ops:
  83.8 1.0 %copy-start = (f32[64,2048]{1,0:T(8,128)S(1)}, f32[64,2048]{1,0:T(8,128)}, u32[]{:S(2)}) copy-start(f32[64,2048]{1,0:T(8,128)} %get-tuple-element.4.ut) | copy-start | bytes 1572868
  84.9 1.0 %copy-start.1 = (f32[64,2048]{1,0:T(8,128)S(1)}, f32[64,2048]{1,0:T(8,128)}, u32[]{:S(2)}) copy-start(f32[64,2048]{1,0:T(8,128)} %get-tuple-element.5.vt) | copy-start | bytes 1572868

commit v3 on v2

--- a/solution.py
+++ b/solution.py
@@ -106,6 +106,13 @@
     def device(gi):
         return {"dp": gi // n_f, "fsdp": gi % n_f}
 
+    barrier = pltpu.get_barrier_semaphore()
+
+    def greet(o, carry):
+        pl.semaphore_signal(barrier, inc=1, device_id=device((g + o) % n_all), device_id_type=MESH)
+        return carry
+
+    lax.fori_loop(1, n_all, greet, 0)
     own = pltpu.make_async_copy(acts, xbuf.at[f], own_sem.at[0])
     own.start()
     ogc = pltpu.make_async_copy(out_grad, og, own_sem.at[1])
@@ -119,13 +126,6 @@
             cp.start()
             weights.append(cp)
 
-    barrier = pltpu.get_barrier_semaphore()
-
-    def greet(o, carry):
-        pl.semaphore_signal(barrier, inc=1, device_id=device((g + o) % n_all), device_id_type=MESH)
-        return carry
-
-    lax.fori_loop(1, n_all, greet, 0)
     pl.semaphore_wait(barrier, n_all - 1)
 
     def push(block, target, send, recv):

time: 92.2 us -> 91.9 us (level)
  no operation moved by 1% of the time
where the time goes in v3:
time: 91.9 us; the launch traced here: 91.6 us
  Pallas kernels  88.9 us (97%)
  local copies, waits for them, and re-layouts  2.08 us (2%)
    pallas_call x1, Pallas kernels, fused(): pl.pallas_call(functools.partial(fused_kernel, n_f, n_dp), out_shape=(jax...  82.8 us
    pallas_call x1, Pallas kernels, fused(): pl.pallas_call(functools.partial(moment_kernel, width, cols, tokens // n_...  6.06 us
    unnamed x4, local copies, waits for them, and re-layouts  2.08 us

profile of v3, /device:TPU:0, one launch (start us, length us, event | category | flops | bytes accessed | tf_op | source)
XLA Modules:
  0.0 91.6 jit_solution(7382324084897604886)
XLA Ops:
  0.6 82.8 %shard_map.77 = (f32[64,2048]{1,0:T(8,128)}, f32[64,2048]{1,0:T(8,128)}) custom-call(bf16[64,4096]{1,0:T(8,128)(2,1)} %acts.1, bf16[64,4096]{1,0:T(8,128)(2,1)} %out_grad.1, bf16[896,4096]{1,0:T(8,128)(2,1)} %gate_w.1, bf16[896,4096]{1,0:T(8,128)(2,1)} %up_w.1, bf16[64,896]{1,0:T(8,128)(2,1)} %bitcast.3, bf16[64,4096]{1,0:T(8,128)(2,1)} %bitcast.2), custom_call_target="tpu_custom_call" | custom-call | tf_op jit(solution)/shard_map/pallas_call | solution.py:363
  83.5 0.0 copy-start
  83.5 1.0 %copy-done = f32[64,2048]{1,0:T(8,128)S(1)} copy-done((f32[64,2048]{1,0:T(8,128)S(1)}, f32[64,2048]{1,0:T(8,128)}, u32[]{:S(2)}) %copy-start) | copy-done | bytes 524312
  84.5 0.0 copy-start.1
  84.5 1.0 %copy-done.1 = f32[64,2048]{1,0:T(8,128)S(1)} copy-done((f32[64,2048]{1,0:T(8,128)S(1)}, f32[64,2048]{1,0:T(8,128)}, u32[]{:S(2)}) %copy-start.1) | copy-done | bytes 524312
  85.6 6.1 %shard_map.78 = (f32[2,256]{1,0:T(2,128)}, f32[256,2048]{1,0:T(8,128)}) custom-call(f32[64,2048]{1,0:T(8,128)S(1)} %copy-done, f32[64,2048]{1,0:T(8,128)S(1)} %copy-done.1), custom_call_target="tpu_custom_call" | custom-call | tf_op jit(solution)/shard_map/pallas_call | solution.py:390
Async XLA Ops:
  83.5 1.0 %copy-start = (f32[64,2048]{1,0:T(8,128)S(1)}, f32[64,2048]{1,0:T(8,128)}, u32[]{:S(2)}) copy-start(f32[64,2048]{1,0:T(8,128)} %get-tuple-element.4.ut) | copy-start | bytes 1572868
  84.5 1.0 %copy-start.1 = (f32[64,2048]{1,0:T(8,128)S(1)}, f32[64,2048]{1,0:T(8,128)}, u32[]{:S(2)}) copy-start(f32[64,2048]{1,0:T(8,128)} %get-tuple-element.5.vt) | copy-start | bytes 1572868
